TPU v7x, 32 devices: a whole 2x2x4 slice. The times are simulated.
32 devices in a mesh: group: 8 (over z, y), tp: 4 (over x, core).
Axes of the slice: x: 2, y: 2, z: 4, core: 2. Of those that a mesh axis runs over, the one named last changes fastest.
Arguments:
- pf_query: bfloat16 [2048, 8192], P('group', 'tp'), may hold values from -16 to 16
- pf_cache: bfloat16 [8, 2, 4096, 1024], P('group', None, 'tp'), may hold values from -16 to 16
- pf_offset: int32 [8], replicated, may hold values from 0 to 3840
- dec_query: bfloat16 [16, 8192], P('group', 'tp'), may hold values from -16 to 16
- dec_cache: bfloat16 [24, 2, 2048, 1024], P('group', None, 'tp'), may hold values from -16 to 16
- slot_owner: int32 [24], replicated, may hold values from 0 to 15, as said below
- slot_len: int32 [24], replicated, may hold values from 1 to 2048
Outputs:
- pf_out: bfloat16 [2048, 8192], P('group', 'tp')
- dec_out: bfloat16 [16, 8192], P('group', 'tp')
Inputs may be any that keep to these rules, and one draw needn't show every extreme that they name: `slot_owner`: every decode request owns one or two slots.
All inputs are finite; a program needn't handle non-finite values.
Results may differ from a plain program's by a relative error of at most 0.005.
Values may be sent and summed in bfloat16 or wider, within the bound.
A program may use at most 128 MiB of HBM per device.

v0:
```python
import jax
import jax.numpy as jnp
from jax import lax
from jax.sharding import PartitionSpec as P

QH = 64
KVH = 8
HD = 128
negative_big = -1e30


def merged_2(value, axis, join):
    pieces = jax.tree.map(lambda part: lax.all_gather(part, axis), value)
    head = jax.tree.map(lambda part: part[0], pieces)
    tail = jax.tree.map(lambda part: part[1:], pieces)
    running, _ = lax.scan(lambda running, share: (join(running, share), None), head, tail)
    return running


def attend_block(queries, cache_keys, cache_values, visible, score_scale):
    scores = (
        jnp.einsum("qgd,nd->gqn", queries, cache_keys, preferred_element_type=jnp.float32)
        * score_scale
    )
    scores = jnp.where(visible[None], scores, negative_big)
    maxima = jnp.max(scores, axis=-1)
    weights = jnp.where(visible[None], jnp.exp(scores - maxima[..., None]), 0.0).astype(
        jnp.bfloat16
    )
    totals = jnp.sum(weights, axis=-1, dtype=jnp.float32)
    weighted = jnp.einsum("gqn,nd->gqd", weights, cache_values, preferred_element_type=jnp.float32)
    return (maxima, totals, weighted)


def merge_along(maxima, totals, weighted, axis):
    largest = jnp.max(maxima, axis=axis, keepdims=True)
    factor = jnp.exp(maxima - largest)
    return (
        jnp.squeeze(largest, axis),
        jnp.sum(totals * factor, axis=axis),
        jnp.sum(weighted * factor[..., None], axis=axis),
    )


def combine_pair(first, second):
    largest = jnp.maximum(first[0], second[0])
    first_factor = jnp.exp(first[0] - largest)
    second_factor = jnp.exp(second[0] - largest)
    return (
        largest,
        first[1] * first_factor + second[1] * second_factor,
        first[2] * first_factor[..., None] + second[2] * second_factor[..., None],
    )


def masked_merge(hits, maxima, totals, weighted):
    selected_picks = jnp.where(hits[:, :, None], maxima[None], negative_big)
    largest = jnp.max(selected_picks, axis=1)
    factor = jnp.where(hits[:, :, None], jnp.exp(selected_picks - largest[:, None]), 0.0)
    denominator = jnp.einsum("abh,bh->ah", factor, totals, precision=lax.Precision.HIGHEST)
    numerator = jnp.einsum("abh,bhd->ahd", factor, weighted, precision=lax.Precision.HIGHEST)
    return (largest, denominator, numerator)


def on_device(pf_query, pf_cache, pf_offset, dec_query, dec_cache, slot_owner, slot_len):
    tp_count = lax.axis_size("tp")
    tp_rank = lax.axis_index("tp")
    group_rank = lax.axis_index("group")
    head_size = HD
    kv_heads = KVH
    width = QH // KVH
    local_heads = QH // tp_count
    score_scale = head_size ** (-0.5)
    pf_rows = pf_query.shape[0]
    local_len = pf_cache.shape[2]
    offset = lax.dynamic_index_in_dim(pf_offset, group_rank, keepdims=False)
    query_pos = offset + jnp.arange(pf_rows, dtype=jnp.int32)
    every_head = lax.all_gather(pf_query, "tp", axis=1, tiled=True)
    grouped = jnp.moveaxis(every_head.reshape(pf_rows, kv_heads, width, head_size), 1, 0)
    cache_keys = jnp.moveaxis(pf_cache[0, 0].reshape(local_len, kv_heads, head_size), 1, 0)
    cache_values = jnp.moveaxis(pf_cache[0, 1].reshape(local_len, kv_heads, head_size), 1, 0)
    key_pos = tp_rank * local_len + jnp.arange(local_len, dtype=jnp.int32)
    visible = key_pos[None, :] <= query_pos[:, None]
    maxima, totals, weighted = lax.map(
        lambda items: attend_block(items[0], items[1], items[2], visible, score_scale),
        (grouped, cache_keys, cache_values),
    )
    maxima = maxima.reshape(tp_count, local_heads, pf_rows)
    totals = totals.reshape(tp_count, local_heads, pf_rows)
    weighted = weighted.reshape(tp_count, local_heads, pf_rows, head_size)
    maxima, totals, weighted = (
        lax.all_to_all(maxima, "tp", split_axis=0, concat_axis=0, tiled=True),
        lax.all_to_all(totals, "tp", split_axis=0, concat_axis=0, tiled=True),
        lax.all_to_all(weighted, "tp", split_axis=0, concat_axis=0, tiled=True),
    )
    largest, denominator, numerator = merge_along(maxima, totals, weighted, 0)
    prefill_heads = numerator / denominator[..., None]
    pf_out = (
        jnp.moveaxis(prefill_heads, 1, 0)
        .reshape(pf_rows, local_heads * head_size)
        .astype(jnp.bfloat16)
    )
    served = dec_query.shape[0]
    head_queries_dec = lax.all_gather(dec_query, "tp", axis=1, tiled=True)
    all_queries = lax.all_gather(head_queries_dec, "group", axis=0, tiled=True)
    slots_here = dec_cache.shape[0]
    slot_local_len = dec_cache.shape[2]
    owners = lax.dynamic_slice_in_dim(slot_owner, group_rank * slots_here, slots_here)
    length_list = lax.dynamic_slice_in_dim(slot_len, group_rank * slots_here, slots_here)
    slot_queries = jnp.take(all_queries, owners, axis=0).reshape(
        slots_here, kv_heads, width, head_size
    )
    slot_keys = dec_cache[:, 0].reshape(slots_here, slot_local_len, kv_heads, head_size)
    slot_values = dec_cache[:, 1].reshape(slots_here, slot_local_len, kv_heads, head_size)
    scores = (
        jnp.einsum("skgd,slkd->skgl", slot_queries, slot_keys, preferred_element_type=jnp.float32)
        * score_scale
    )
    slot_pos = tp_rank * slot_local_len + jnp.arange(slot_local_len, dtype=jnp.int32)
    live = (slot_pos[None, :] < length_list[:, None])[:, None, None, :]
    scores = jnp.where(live, scores, negative_big)
    slot_max = jnp.max(scores, axis=-1)
    slot_weights = jnp.where(live, jnp.exp(scores - slot_max[..., None]), 0.0).astype(jnp.bfloat16)
    slot_totals = jnp.sum(slot_weights, axis=-1, dtype=jnp.float32)
    slot_weighted = jnp.einsum(
        "skgl,slkd->skgd", slot_weights, slot_values, preferred_element_type=jnp.float32
    )
    slot_max = slot_max.reshape(slots_here, QH)
    slot_totals = slot_totals.reshape(slots_here, QH)
    slot_weighted = slot_weighted.reshape(slots_here, QH, head_size)
    merged = merged_2((slot_max, slot_totals, slot_weighted), "tp", combine_pair)
    head_max = lax.dynamic_slice_in_dim(merged[0], tp_rank * local_heads, local_heads, 1)
    head_totals = lax.dynamic_slice_in_dim(merged[1], tp_rank * local_heads, local_heads, 1)
    head_weighted = lax.dynamic_slice_in_dim(merged[2], tp_rank * local_heads, local_heads, 1)
    every_max, every_totals, every_weighted = (
        lax.all_gather(head_max, "group", axis=0, tiled=True),
        lax.all_gather(head_totals, "group", axis=0, tiled=True),
        lax.all_gather(head_weighted, "group", axis=0, tiled=True),
    )
    mine = group_rank * served + jnp.arange(served, dtype=jnp.int32)
    hits = slot_owner[None, :] == mine[:, None]
    largest_dec, denominator_dec, numerator_dec = masked_merge(
        hits, every_max, every_totals, every_weighted
    )
    dec_out = (
        (numerator_dec / denominator_dec[..., None])
        .reshape(served, local_heads * head_size)
        .astype(jnp.bfloat16)
    )
    return (pf_out, dec_out)


def solution(mesh):
    placed = (
        P("group", "tp"),
        P("group", None, "tp", None),
        P(),
        P("group", "tp"),
        P("group", None, "tp", None),
        P(),
        P(),
    )
    return jax.shard_map(
        on_device,
        mesh=mesh,
        in_specs=placed,
        out_specs=(P("group", "tp"), P("group", "tp")),
        check_vma=False,
    )
```

profile of v0, /device:TPU:0, one launch (start us, length us, event | category | flops | bytes accessed | tf_op | source)
XLA Modules:
  0.0 403.5 jit_solution(4472428663473686276)
XLA Ops:
  9.5 4.0 fusion.46
  13.5 4.0 copy.61
  21.2 26.1 %all-gather.5.cloned.1.call-done = bf16[256,8192]{0,1:T(8,128)(2,1)} async-done(((bf16[256,2048]{0,1:T(8,128)(2,1)}), bf16[256,8192]{0,1:T(8,128)(2,1)}) %all-gather.5.cloned.1.call-update) | async-done | bytes 4194320 | tf_op jit(solution)/shard_map/all_gather | solution.py:78
  47.3 74.8 %while.30 = (s32[]{:T(128)}, f32[8,8,256]{2,1,0:T(8,128)S(1)}, f32[8,8,256]{2,1,0:T(8,128)S(1)}, f32[8,8,256,128]{3,2,1,0:T(8,128)}, bf16[8,1024,128]{1,2,0:T(8,...) while((s32[]{:T(128)}, f32[8,8,256]{2,1,0:T(8,128)S(1)}, ...), condition=%wide.region_3.4_spmd.clone, body=%wide.region_0.3_spmd.clone.sunk | while | flops 1105457152 | bytes 28384368 | solution.py:84
  47.6 2.6 fusion.59
  52.2 4.6 %fusion.60 = f32[8,8,256,128]{3,2,1,0:T(8,128)} fusion(f32[8,8,256,128]{3,2,1,0:T(8,128)} %get-tuple-element.319, s32[]{:T(128)S(6)} %copy.81, bf16[8,1024,128]{1,2,0:T(8,128)(2,1)} %get-tuple-element.332, f32[1024,256,8]{1,0,2:T(8,128)S(1)} %get-tuple-element.303, f32[8,256]{1,0:T(8,128)S(1)} %get-tuple-element.302, ...), kind=kOutput, calls=%fused_computation.15.clone.1 | convolution fusion | flops 547356672 | bytes 9970688 | tf_op jit(solution)/shard_map/while/body/eval_jaxpr/gqn,nd->gqd/dot_general | solution.py:31
  61.6 4.5 %fusion.60 = f32[8,8,256,128]{3,2,1,0:T(8,128)} fusion(f32[8,8,256,128]{3,2,1,0:T(8,128)} %get-tuple-element.319, s32[]{:T(128)S(6)} %copy.81, bf16[8,1024,128]{1,2,0:T(8,128)(2,1)} %get-tuple-element.332, f32[1024,256,8]{1,0,2:T(8,128)S(1)} %get-tuple-element.303, f32[8,256]{1,0:T(8,128)S(1)} %get-tuple-element.302, ...), kind=kOutput, calls=%fused_computation.15.clone.1 | convolution fusion | flops 547356672 | bytes 9970688 | tf_op jit(solution)/shard_map/while/body/eval_jaxpr/gqn,nd->gqd/dot_general | solution.py:31
  66.3 2.6 fusion.59
  70.9 4.5 %fusion.60 = f32[8,8,256,128]{3,2,1,0:T(8,128)} fusion(f32[8,8,256,128]{3,2,1,0:T(8,128)} %get-tuple-element.319, s32[]{:T(128)S(6)} %copy.81, bf16[8,1024,128]{1,2,0:T(8,128)(2,1)} %get-tuple-element.332, f32[1024,256,8]{1,0,2:T(8,128)S(1)} %get-tuple-element.303, f32[8,256]{1,0:T(8,128)S(1)} %get-tuple-element.302, ...), kind=kOutput, calls=%fused_computation.15.clone.1 | convolution fusion | flops 547356672 | bytes 9970688 | tf_op jit(solution)/shard_map/while/body/eval_jaxpr/gqn,nd->gqd/dot_general | solution.py:31
  75.6 2.6 fusion.59
  80.3 4.5 %fusion.60 = f32[8,8,256,128]{3,2,1,0:T(8,128)} fusion(f32[8,8,256,128]{3,2,1,0:T(8,128)} %get-tuple-element.319, s32[]{:T(128)S(6)} %copy.81, bf16[8,1024,128]{1,2,0:T(8,128)(2,1)} %get-tuple-element.332, f32[1024,256,8]{1,0,2:T(8,128)S(1)} %get-tuple-element.303, f32[8,256]{1,0:T(8,128)S(1)} %get-tuple-element.302, ...), kind=kOutput, calls=%fused_computation.15.clone.1 | convolution fusion | flops 547356672 | bytes 9970688 | tf_op jit(solution)/shard_map/while/body/eval_jaxpr/gqn,nd->gqd/dot_general | solution.py:31
  89.6 4.5 %fusion.60 = f32[8,8,256,128]{3,2,1,0:T(8,128)} fusion(f32[8,8,256,128]{3,2,1,0:T(8,128)} %get-tuple-element.319, s32[]{:T(128)S(6)} %copy.81, bf16[8,1024,128]{1,2,0:T(8,128)(2,1)} %get-tuple-element.332, f32[1024,256,8]{1,0,2:T(8,128)S(1)} %get-tuple-element.303, f32[8,256]{1,0:T(8,128)S(1)} %get-tuple-element.302, ...), kind=kOutput, calls=%fused_computation.15.clone.1 | convolution fusion | flops 547356672 | bytes 9970688 | tf_op jit(solution)/shard_map/while/body/eval_jaxpr/gqn,nd->gqd/dot_general | solution.py:31
  94.3 2.6 fusion.59
  99.0 4.5 %fusion.60 = f32[8,8,256,128]{3,2,1,0:T(8,128)} fusion(f32[8,8,256,128]{3,2,1,0:T(8,128)} %get-tuple-element.319, s32[]{:T(128)S(6)} %copy.81, bf16[8,1024,128]{1,2,0:T(8,128)(2,1)} %get-tuple-element.332, f32[1024,256,8]{1,0,2:T(8,128)S(1)} %get-tuple-element.303, f32[8,256]{1,0:T(8,128)S(1)} %get-tuple-element.302, ...), kind=kOutput, calls=%fused_computation.15.clone.1 | convolution fusion | flops 547356672 | bytes 9970688 | tf_op jit(solution)/shard_map/while/body/eval_jaxpr/gqn,nd->gqd/dot_general | solution.py:31
  103.7 2.6 fusion.59
  108.3 4.5 %fusion.60 = f32[8,8,256,128]{3,2,1,0:T(8,128)} fusion(f32[8,8,256,128]{3,2,1,0:T(8,128)} %get-tuple-element.319, s32[]{:T(128)S(6)} %copy.81, bf16[8,1024,128]{1,2,0:T(8,128)(2,1)} %get-tuple-element.332, f32[1024,256,8]{1,0,2:T(8,128)S(1)} %get-tuple-element.303, f32[8,256]{1,0:T(8,128)S(1)} %get-tuple-element.302, ...), kind=kOutput, calls=%fused_computation.15.clone.1 | convolution fusion | flops 547356672 | bytes 9970688 | tf_op jit(solution)/shard_map/while/body/eval_jaxpr/gqn,nd->gqd/dot_general | solution.py:31
  117.6 4.5 %fusion.60 = f32[8,8,256,128]{3,2,1,0:T(8,128)} fusion(f32[8,8,256,128]{3,2,1,0:T(8,128)} %get-tuple-element.319, s32[]{:T(128)S(6)} %copy.81, bf16[8,1024,128]{1,2,0:T(8,128)(2,1)} %get-tuple-element.332, f32[1024,256,8]{1,0,2:T(8,128)S(1)} %get-tuple-element.303, f32[8,256]{1,0:T(8,128)S(1)} %get-tuple-element.302, ...), kind=kOutput, calls=%fused_computation.15.clone.1 | convolution fusion | flops 547356672 | bytes 9970688 | tf_op jit(solution)/shard_map/while/body/eval_jaxpr/gqn,nd->gqd/dot_general | solution.py:31
  122.1 7.1 %all_to_all.15 = f32[4,16,256]{2,1,0:T(8,128)} all-to-all(f32[4,16,256]{2,1,0:T(8,128)S(1)} %bitcast.139), channel_id=1, replica_groups=mesh['group'=8,'tp'=4] {'tp'}, dimensions={0} | all-to-all | bytes 131072 | tf_op jit(solution)/shard_map/all_to_all | solution.py:93
  129.2 7.1 %all_to_all.16 = f32[4,16,256]{2,1,0:T(8,128)} all-to-all(f32[4,16,256]{2,1,0:T(8,128)S(1)} %bitcast.138), channel_id=1, replica_groups=mesh['group'=8,'tp'=4] {'tp'}, dimensions={0} | all-to-all | bytes 131072 | tf_op jit(solution)/shard_map/all_to_all | solution.py:92
  136.4 5.7 %all-to-all-start = ((f32[4,16,256,128]{3,2,1,0:T(8,128)}), f32[4,16,256,128]{3,2,1,0:T(8,128)}, u32[]{:S(2)}, u32[]{:S(2)}) async-start(f32[4,16,256,128]{3,2,1,0:T(8,128)} %bitcast.130), calls=%async_computation | async-start | bytes 16777216 | tf_op jit(solution)/shard_map/all_to_all | solution.py:94
  142.1 6.9 %fusion.45 = (bf16[3,1,512,1024]{3,2,1,0:T(8,128)(2,1)}, bf16[3,1,512,1024]{3,2,1,0:T(8,128)(2,1)}) fusion(bf16[3,2,512,1024]{3,2,1,0:T(8,128)(2,1)} %param.15), kind=kLoop, calls=%fused_computation.81 | loop fusion | bytes 12582912 | tf_op jit(solution)/shard_map/slice | solution.py:114
  149.0 3.2 copy.63
  152.2 84.0 %all_gather.28 = bf16[2,8192]{1,0:T(2,128)(2,1)S(1)} all-gather(bf16[2,2048]{1,0:T(2,128)(2,1)S(1)} %copy-done.2), channel_id=1, replica_groups=mesh['group'=8,'tp'=4] {'tp'}, dimensions={1}, use_global_device_ids=true | all-gather | bytes 40960 | tf_op jit(solution)/shard_map/all_gather | solution.py:104
  236.2 32.8 %all-gather = bf16[8,2,8192]{2,1,0:T(2,128)(2,1)} all-gather(bf16[1,2,8192]{2,1,0:T(2,128)(2,1)S(1)} %bitcast.136), channel_id=1, replica_groups=mesh['group'=8,'tp'=4] {'group'}, dimensions={0}, use_global_device_ids=true | all-gather | bytes 294912 | tf_op jit(solution)/shard_map/all_gather | solution.py:105
  275.1 3.2 copy.64
  278.3 5.3 %all_gather.30 = f32[4,3,64]{2,1,0:T(4,128)S(1)} all-gather(f32[1,3,64]{2,1,0:T(4,128)} %all_gather_reshape.9), channel_id=1, replica_groups=mesh['group'=8,'tp'=4] {'tp'}, dimensions={0}, use_global_device_ids=true | all-gather | bytes 3840 | tf_op jit(solution)/shard_map/all_gather | solution.py:13
  284.2 5.3 %all_gather.31 = f32[4,3,64]{2,1,0:T(4,128)S(1)} all-gather(f32[1,3,64]{2,1,0:T(4,128)} %all_gather_reshape.10), channel_id=1, replica_groups=mesh['group'=8,'tp'=4] {'tp'}, dimensions={0}, use_global_device_ids=true | all-gather | bytes 3840 | tf_op jit(solution)/shard_map/all_gather | solution.py:13
  291.0 6.5 %all_gather.32 = f32[4,3,64,128]{3,2,1,0:T(8,128)S(1)} all-gather(f32[1,3,64,128]{3,2,1,0:T(8,128)S(1)} %convolution_bitcast_fusion.1), channel_id=1, replica_groups=mesh['group'=8,'tp'=4] {'tp'}, dimensions={0}, use_global_device_ids=true | all-gather | bytes 491520 | tf_op jit(solution)/shard_map/all_gather | solution.py:13
  301.6 26.0 %all-gather.2 = f32[8,3,16]{2,1,0:T(4,128)S(1)} all-gather(f32[1,3,16]{2,1,0:T(4,128)S(1)} %dynamic-slice_bitcast_fusion), channel_id=1, replica_groups=mesh['group'=8,'tp'=4] {'group'}, dimensions={0}, use_global_device_ids=true | all-gather | bytes 1728 | tf_op jit(solution)/shard_map/all_gather | solution.py:137
  327.8 26.2 %all-gather.1 = f32[8,3,16]{2,1,0:T(4,128)S(1)} all-gather(f32[1,3,16]{2,1,0:T(4,128)S(1)} %dynamic-slice_bitcast_fusion.1), channel_id=1, replica_groups=mesh['group'=8,'tp'=4] {'group'}, dimensions={0}, use_global_device_ids=true | all-gather | bytes 1728 | tf_op jit(solution)/shard_map/all_gather | solution.py:136
  354.0 30.6 %all_gather.33 = f32[24,16,128]{2,1,0:T(8,128)S(1)} all-gather(f32[3,16,128]{2,1,0:T(8,128)S(1)} %constant_dynamic-slice_fusion), channel_id=1, replica_groups=mesh['group'=8,'tp'=4] {'group'}, dimensions={0}, use_global_device_ids=true | all-gather | bytes 221184 | tf_op jit(solution)/shard_map/all_gather | solution.py:138
  388.5 5.4 %multiply_reduce_fusion = f32[16,256,128]{2,1,0:T(8,128)S(1)} fusion(f32[4,16,256,128]{3,2,1,0:T(8,128)} %all-to-all-done, f32[4,16,256]{2,1,0:T(8,128)S(1)} %get-tuple-element.181), kind=kLoop, calls=%fused_computation.28 | loop fusion | flops 3670016 | bytes 10551296 | tf_op jit(solution)/shard_map/reduce_sum | solution.py:41
  (92 shorter events, 53.2 us)
Async XLA Ops:
  7.2 40.2 %all-gather.5.cloned.1.call-start = ((), (), s32[]{:S(2)}) async-start(), calls=%async_computation.3 | async-start | bytes 5242880 | tf_op jit(solution)/shard_map/all_gather | solution.py:78
  13.5 6.5 %copy-start.4 = (s32[8]{0:T(128)S(1)}, s32[8]{0:T(128)}, u32[]{:S(2)}) copy-start(s32[8]{0:T(128)} %param.13) | copy-start | bytes 100
  136.4 252.1 %all-to-all-start = ((f32[4,16,256,128]{3,2,1,0:T(8,128)}), f32[4,16,256,128]{3,2,1,0:T(8,128)}, u32[]{:S(2)}, u32[]{:S(2)}) async-start(f32[4,16,256,128]{3,2,1,0:T(8,128)} %bitcast.130), calls=%async_computation | async-start | bytes 16777216 | tf_op jit(solution)/shard_map/all_to_all | solution.py:94
  149.0 3.2 copy-start.2
  149.0 121.1 %copy-start.5 = (s32[24]{0:T(128)S(1)}, s32[24]{0:T(128)}, u32[]{:S(2)}) copy-start(s32[24]{0:T(128)} %param.17) | copy-start | bytes 292
  149.0 121.2 %copy-start.3 = (s32[24]{0:T(128)S(1)}, s32[24]{0:T(128)}, u32[]{:S(2)}) copy-start(s32[24]{0:T(128)} %param.16) | copy-start | bytes 292
  283.6 6.5 %copy-start = (f32[4,3,64]{2,1,0:T(4,128)}, f32[4,3,64]{2,1,0:T(4,128)S(1)}, u32[]{:S(2)}) copy-start(f32[4,3,64]{2,1,0:T(4,128)S(1)} %all_gather.30) | copy-start | bytes 9220
  289.4 0.6 copy-start.1
Sparse Core Ops, SparseCore 0:
  10.1 37.1 all-gather.4
where the time goes:
time: 405 us; the launch traced here: 403 us
  blocking collectives  231 us (57%)
  matrix products  60.3 us (15%)
  local copies, waits for them, and re-layouts  35.3 us (9%)
  other arithmetic  30.4 us (8%)
  waiting for transfers between devices  26.1 us (6%)
  between operations  14.2 us (4%)
  starting transfers between devices  5.69 us (1%)
    all_gather x1, blocking collectives, on_device(): head_queries_dec = lax.all_gather(dec_query, 'tp', axis=1, tiled=True)  84 us
    dot_general x8, matrix products, attend_block(): jnp.einsum('gqn,nd->gqd', weights, cache_values, preferred_element_type=j...  35.9 us
    all_gather x1, blocking collectives, on_device(): all_queries = lax.all_gather(head_queries_dec, 'group', axis=0, tiled=True)  32.8 us
    all_gather x1, blocking collectives, on_device(): lax.all_gather(head_weighted, 'group', axis=0, tiled=True)  30.6 us
    all_gather x1, blocking collectives, on_device(): lax.all_gather(head_max, 'group', axis=0, tiled=True)  26.2 us
    all_gather x1, waiting for transfers between devices, on_device(): every_head = lax.all_gather(pf_query, 'tp', axis=1, tiled=True)  26.1 us
    all_gather x1, blocking collectives, on_device(): lax.all_gather(head_totals, 'group', axis=0, tiled=True)  26 us
    dot_general x8, matrix products, attend_block(): jnp.einsum('qgd,nd->gqn', queries, cache_keys, preferred_element_type=jnp...  20.8 us
  transfers between devices with their start and end apart: 2, of which 1 were waited for; matrix products, arithmetic and copies ran while one was open for 10% of the time, Pallas kernels for 0%

commit v1 on v0

--- a/solution.py
+++ b/solution.py
@@ -101,7 +101,12 @@
         .astype(jnp.bfloat16)
     )
     served = dec_query.shape[0]
-    head_queries_dec = lax.all_gather(dec_query, "tp", axis=1, tiled=True)
+    ring = [dec_query]
+    for hop in range(3):
+        ring.append(lax.ppermute(ring[-1], "tp", [(dev, (dev + 1) % 4) for dev in range(4)]))
+    head_queries_dec = jnp.roll(
+        jnp.concatenate(ring[::-1], axis=1), (lax.axis_index("tp") + 1) * ring[0].shape[1], axis=1
+    )
     all_queries = lax.all_gather(head_queries_dec, "group", axis=0, tiled=True)
     slots_here = dec_cache.shape[0]
     slot_local_len = dec_cache.shape[2]

time: 405 us -> 360 us (0.89)
  blocking collectives: 231 us -> 184 us
  waiting for transfers between devices: 26.1 us -> 15.6 us
  starting transfers between devices: 5.69 us -> 15.8 us
    all_gather x1 -> x0, blocking collectives: 84 us -> none  [on_device(): head_queries_dec = lax.all_gather(dec_query, 'tp', axis=1, tiled=True)]
    all_gather x3, blocking collectives: 17.1 us -> 68.6 us  [merged_2(): pieces = jax.tree.map(lambda part: lax.all_gather(part, axis), value)]
    all_gather x1, waiting for transfers between devices: 26.1 us -> 7.45 us  [on_device(): every_head = lax.all_gather(pf_query, 'tp', axis=1, tiled=True)]
    all_to_all x2 -> x0, blocking collectives: 14.3 us -> none  [the longest x1 7.15 us: on_device(): lax.all_to_all(maxima, 'tp', split_axis=0, concat_axis=0, tiled=True)]
    all_to_all x0 -> x2, waiting for transfers between devices: none -> 8.13 us  [the longest x1 4.07 us: on_device(): lax.all_to_all(maxima, 'tp', split_axis=0, concat_axis=0, tiled=True)]
    all_to_all x0 -> x2, starting transfers between devices: none -> 6.56 us  [the longest x1 3.28 us: on_device(): lax.all_to_all(totals, 'tp', split_axis=0, concat_axis=0, tiled=True)]
    dynamic_update_slice x8, local copies, waits for them, and re-layouts: 0.07 us -> 4.88 us  [on_device(): lax.map(lambda items: attend_block(items[0], items[1], items[2], visible,...]
    unnamed x25 -> x37, local copies, waits for them, and re-layouts: 18 us -> 20.9 us
  transfers between devices with their start and end apart: 2 -> 7, of which waited for: 1 -> 3; matrix products, arithmetic and copies ran while one was open for 10% -> 33% of each run, Pallas kernels for 0% -> 0%
where the time goes in v1:
time: 360 us; the launch traced here: 359 us
  blocking collectives  184 us (51%)
  matrix products  62.8 us (17%)
  local copies, waits for them, and re-layouts  36.8 us (10%)
  other arithmetic  28.9 us (8%)
  starting transfers between devices  15.8 us (4%)
  waiting for transfers between devices  15.6 us (4%)
  between operations  14.3 us (4%)
    all_gather x3, blocking collectives, merged_2(): pieces = jax.tree.map(lambda part: lax.all_gather(part, axis), value)  68.6 us
    dot_general x8, matrix products, attend_block(): jnp.einsum('gqn,nd->gqd', weights, cache_values, preferred_element_type=j...  35.8 us
    all_gather x1, blocking collectives, on_device(): all_queries = lax.all_gather(head_queries_dec, 'group', axis=0, tiled=True)  32.8 us
    all_gather x1, blocking collectives, on_device(): lax.all_gather(head_weighted, 'group', axis=0, tiled=True)  30.6 us
    all_gather x1, blocking collectives, on_device(): lax.all_gather(head_totals, 'group', axis=0, tiled=True)  26.2 us
    all_gather x1, blocking collectives, on_device(): lax.all_gather(head_max, 'group', axis=0, tiled=True)  26 us
    unnamed x37, local copies, waits for them, and re-layouts  20.9 us
    dot_general x8, matrix products, attend_block(): jnp.einsum('qgd,nd->gqn', queries, cache_keys, preferred_element_type=jnp...  20.8 us
  transfers between devices with their start and end apart: 7, of which 3 were waited for; matrix products, arithmetic and copies ran while one was open for 33% of the time, Pallas kernels for 0%

profile of v1, /device:TPU:0, one launch (start us, length us, event | category | flops | bytes accessed | tf_op | source)
XLA Modules:
  0.0 358.6 jit_solution(10446828984978401989)
XLA Ops:
  13.7 4.0 %fusion.46 = (bf16[1,1,1024,1024]{3,2,1,0:T(8,128)(2,1)S(1)}, bf16[1,1,1024,1024]{3,2,1,0:T(8,128)(2,1)}) fusion(bf16[1,2,1024,1024]{3,2,1,0:T(8,128)(2,1)} %param.12), kind=kLoop, calls=%fused_computation.91 | loop fusion | bytes 8388608 | tf_op jit(solution)/shard_map/slice | solution.py:81
  17.7 3.5 fusion.45
  25.2 4.0 %copy.61 = bf16[1,1,1024,1024]{2,3,1,0:T(8,128)(2,1)} copy(bf16[1,1,1024,1024]{3,2,1,0:T(8,128)(2,1)} %get-tuple-element.189) | data formatting | bytes 4194304
  31.7 3.2 copy.63
  34.9 4.7 %copy.64 = bf16[3,1,512,1024]{2,3,0,1:T(8,128)(2,1)} copy(bf16[3,1,512,1024]{3,2,1,0:T(8,128)(2,1)} %get-tuple-element.186) | data formatting | bytes 6291456
  40.1 7.5 %all-gather.5.cloned.1.call-done = bf16[256,8192]{0,1:T(8,128)(2,1)} async-done(((bf16[256,2048]{0,1:T(8,128)(2,1)}), bf16[256,8192]{0,1:T(8,128)(2,1)}) %all-gather.5.cloned.1.call-update) | async-done | bytes 4194320 | tf_op jit(solution)/shard_map/all_gather | solution.py:78
  47.5 79.4 %while.30 = (s32[]{:T(128)}, f32[8,8,256]{2,1,0:T(8,128)}, f32[8,8,256]{2,1,0:T(8,128)}, f32[8,8,256,128]{3,2,1,0:T(8,128)}, bf16[8,1024,128]{1,2,0:T(8,128)(2,1...) while((s32[]{:T(128)}, f32[8,8,256]{2,1,0:T(8,128)}, ...), condition=%wide.region_3.4_spmd.clone, body=%wide.region_0.3_spmd.clone.sunk | while | flops 1105457152 | bytes 28384368 | solution.py:84
  53.0 4.5 %fusion.60 = f32[8,8,256,128]{3,2,1,0:T(8,128)} fusion(f32[8,8,256,128]{3,2,1,0:T(8,128)} %get-tuple-element.319, s32[]{:T(128)S(6)} %copy.81, bf16[8,1024,128]{1,2,0:T(8,128)(2,1)} %get-tuple-element.332, f32[1024,256,8]{1,0,2:T(8,128)S(1)} %get-tuple-element.303, f32[8,256]{1,0:T(8,128)S(1)} %get-tuple-element.302, ...), kind=kOutput, calls=%fused_computation.15.clone.1 | convolution fusion | flops 547356672 | bytes 9970688 | tf_op jit(solution)/shard_map/while/body/eval_jaxpr/gqn,nd->gqd/dot_general | solution.py:31
  57.7 2.6 fusion.59
  63.0 4.4 %fusion.60 = f32[8,8,256,128]{3,2,1,0:T(8,128)} fusion(f32[8,8,256,128]{3,2,1,0:T(8,128)} %get-tuple-element.319, s32[]{:T(128)S(6)} %copy.81, bf16[8,1024,128]{1,2,0:T(8,128)(2,1)} %get-tuple-element.332, f32[1024,256,8]{1,0,2:T(8,128)S(1)} %get-tuple-element.303, f32[8,256]{1,0:T(8,128)S(1)} %get-tuple-element.302, ...), kind=kOutput, calls=%fused_computation.15.clone.1 | convolution fusion | flops 547356672 | bytes 9970688 | tf_op jit(solution)/shard_map/while/body/eval_jaxpr/gqn,nd->gqd/dot_general | solution.py:31
  67.6 2.6 fusion.59
  72.9 4.4 %fusion.60 = f32[8,8,256,128]{3,2,1,0:T(8,128)} fusion(f32[8,8,256,128]{3,2,1,0:T(8,128)} %get-tuple-element.319, s32[]{:T(128)S(6)} %copy.81, bf16[8,1024,128]{1,2,0:T(8,128)(2,1)} %get-tuple-element.332, f32[1024,256,8]{1,0,2:T(8,128)S(1)} %get-tuple-element.303, f32[8,256]{1,0:T(8,128)S(1)} %get-tuple-element.302, ...), kind=kOutput, calls=%fused_computation.15.clone.1 | convolution fusion | flops 547356672 | bytes 9970688 | tf_op jit(solution)/shard_map/while/body/eval_jaxpr/gqn,nd->gqd/dot_general | solution.py:31
  82.8 4.5 %fusion.60 = f32[8,8,256,128]{3,2,1,0:T(8,128)} fusion(f32[8,8,256,128]{3,2,1,0:T(8,128)} %get-tuple-element.319, s32[]{:T(128)S(6)} %copy.81, bf16[8,1024,128]{1,2,0:T(8,128)(2,1)} %get-tuple-element.332, f32[1024,256,8]{1,0,2:T(8,128)S(1)} %get-tuple-element.303, f32[8,256]{1,0:T(8,128)S(1)} %get-tuple-element.302, ...), kind=kOutput, calls=%fused_computation.15.clone.1 | convolution fusion | flops 547356672 | bytes 9970688 | tf_op jit(solution)/shard_map/while/body/eval_jaxpr/gqn,nd->gqd/dot_general | solution.py:31
  92.7 4.5 %fusion.60 = f32[8,8,256,128]{3,2,1,0:T(8,128)} fusion(f32[8,8,256,128]{3,2,1,0:T(8,128)} %get-tuple-element.319, s32[]{:T(128)S(6)} %copy.81, bf16[8,1024,128]{1,2,0:T(8,128)(2,1)} %get-tuple-element.332, f32[1024,256,8]{1,0,2:T(8,128)S(1)} %get-tuple-element.303, f32[8,256]{1,0:T(8,128)S(1)} %get-tuple-element.302, ...), kind=kOutput, calls=%fused_computation.15.clone.1 | convolution fusion | flops 547356672 | bytes 9970688 | tf_op jit(solution)/shard_map/while/body/eval_jaxpr/gqn,nd->gqd/dot_general | solution.py:31
  97.4 2.6 fusion.59
  102.7 4.5 %fusion.60 = f32[8,8,256,128]{3,2,1,0:T(8,128)} fusion(f32[8,8,256,128]{3,2,1,0:T(8,128)} %get-tuple-element.319, s32[]{:T(128)S(6)} %copy.81, bf16[8,1024,128]{1,2,0:T(8,128)(2,1)} %get-tuple-element.332, f32[1024,256,8]{1,0,2:T(8,128)S(1)} %get-tuple-element.303, f32[8,256]{1,0:T(8,128)S(1)} %get-tuple-element.302, ...), kind=kOutput, calls=%fused_computation.15.clone.1 | convolution fusion | flops 547356672 | bytes 9970688 | tf_op jit(solution)/shard_map/while/body/eval_jaxpr/gqn,nd->gqd/dot_general | solution.py:31
  112.6 4.5 %fusion.60 = f32[8,8,256,128]{3,2,1,0:T(8,128)} fusion(f32[8,8,256,128]{3,2,1,0:T(8,128)} %get-tuple-element.319, s32[]{:T(128)S(6)} %copy.81, bf16[8,1024,128]{1,2,0:T(8,128)(2,1)} %get-tuple-element.332, f32[1024,256,8]{1,0,2:T(8,128)S(1)} %get-tuple-element.303, f32[8,256]{1,0:T(8,128)S(1)} %get-tuple-element.302, ...), kind=kOutput, calls=%fused_computation.15.clone.1 | convolution fusion | flops 547356672 | bytes 9970688 | tf_op jit(solution)/shard_map/while/body/eval_jaxpr/gqn,nd->gqd/dot_general | solution.py:31
  122.5 4.5 %fusion.60 = f32[8,8,256,128]{3,2,1,0:T(8,128)} fusion(f32[8,8,256,128]{3,2,1,0:T(8,128)} %get-tuple-element.319, s32[]{:T(128)S(6)} %copy.81, bf16[8,1024,128]{1,2,0:T(8,128)(2,1)} %get-tuple-element.332, f32[1024,256,8]{1,0,2:T(8,128)S(1)} %get-tuple-element.303, f32[8,256]{1,0:T(8,128)S(1)} %get-tuple-element.302, ...), kind=kOutput, calls=%fused_computation.15.clone.1 | convolution fusion | flops 547356672 | bytes 9970688 | tf_op jit(solution)/shard_map/while/body/eval_jaxpr/gqn,nd->gqd/dot_general | solution.py:31
  127.0 3.3 all-to-all-start.2
  130.3 4.1 %all-to-all-done.2 = f32[4,16,256]{2,1,0:T(8,128)S(1)} async-done(((f32[4,16,256]{2,1,0:T(8,128)}), f32[4,16,256]{2,1,0:T(8,128)S(1)}, u32[]{:S(2)}, u32[]{:S(2)}) %all-to-all-start.2) | async-done | bytes 65568 | tf_op jit(solution)/shard_map/all_to_all | solution.py:93
  135.0 3.3 all-to-all-start.1
  138.3 4.1 %all-to-all-done.1 = f32[4,16,256]{2,1,0:T(8,128)S(1)} async-done(((f32[4,16,256]{2,1,0:T(8,128)}), f32[4,16,256]{2,1,0:T(8,128)S(1)}, u32[]{:S(2)}, u32[]{:S(2)}) %all-to-all-start.1) | async-done | bytes 65568 | tf_op jit(solution)/shard_map/all_to_all | solution.py:92
  143.0 5.7 %all-to-all-start = ((f32[4,16,256,128]{3,2,1,0:T(8,128)}), f32[4,16,256,128]{3,2,1,0:T(8,128)}, u32[]{:S(2)}, u32[]{:S(2)}) async-start(f32[4,16,256,128]{3,2,1,0:T(8,128)} %bitcast.131), calls=%async_computation | async-start | bytes 16777216 | tf_op jit(solution)/shard_map/all_to_all | solution.py:94
  148.8 32.8 %all-gather = bf16[8,2,8192]{2,1,0:T(2,128)(2,1)} all-gather(bf16[1,2,8192]{2,1,0:T(2,128)(2,1)S(1)} %dynamic-slice_bitcast_fusion), channel_id=1, replica_groups=mesh['group'=8,'tp'=4] {'group'}, dimensions={0}, use_global_device_ids=true | all-gather | bytes 294912 | tf_op jit(solution)/shard_map/all_gather | solution.py:110
  185.8 56.9 %all_gather.26 = f32[4,3,64]{2,1,0:T(4,128)S(1)} all-gather(f32[1,3,64]{2,1,0:T(4,128)S(1)} %all_gather_reshape.9), channel_id=1, replica_groups=mesh['group'=8,'tp'=4] {'tp'}, dimensions={0}, use_global_device_ids=true | all-gather | bytes 3840 | tf_op jit(solution)/shard_map/all_gather | solution.py:13
  242.7 5.1 %all_gather.27 = f32[4,3,64]{2,1,0:T(4,128)S(1)} all-gather(f32[1,3,64]{2,1,0:T(4,128)S(1)} %all_gather_reshape.10), channel_id=1, replica_groups=mesh['group'=8,'tp'=4] {'tp'}, dimensions={0}, use_global_device_ids=true | all-gather | bytes 3840 | tf_op jit(solution)/shard_map/all_gather | solution.py:13
  247.8 2.8 convolution_bitcast_fusion.1
  250.7 6.5 %all_gather.28 = f32[4,3,64,128]{3,2,1,0:T(8,128)S(1)} all-gather(f32[1,3,64,128]{3,2,1,0:T(8,128)S(1)} %convolution_bitcast_fusion.1), channel_id=1, replica_groups=mesh['group'=8,'tp'=4] {'tp'}, dimensions={0}, use_global_device_ids=true | all-gather | bytes 491520 | tf_op jit(solution)/shard_map/all_gather | solution.py:13
  257.9 26.2 %all-gather.2 = f32[8,3,16]{2,1,0:T(4,128)S(1)} all-gather(f32[1,3,16]{2,1,0:T(4,128)S(1)} %dynamic-slice_bitcast_fusion.1), channel_id=1, replica_groups=mesh['group'=8,'tp'=4] {'group'}, dimensions={0}, use_global_device_ids=true | all-gather | bytes 1728 | tf_op jit(solution)/shard_map/all_gather | solution.py:142
  284.3 26.0 %all-gather.1 = f32[8,3,16]{2,1,0:T(4,128)S(1)} all-gather(f32[1,3,16]{2,1,0:T(4,128)S(1)} %dynamic-slice_bitcast_fusion.2), channel_id=1, replica_groups=mesh['group'=8,'tp'=4] {'group'}, dimensions={0}, use_global_device_ids=true | all-gather | bytes 1728 | tf_op jit(solution)/shard_map/all_gather | solution.py:141
  310.4 30.6 %all_gather.29 = f32[24,16,128]{2,1,0:T(8,128)S(1)} all-gather(f32[3,16,128]{2,1,0:T(8,128)S(1)} %constant_dynamic-slice_fusion), channel_id=1, replica_groups=mesh['group'=8,'tp'=4] {'group'}, dimensions={0}, use_global_device_ids=true | all-gather | bytes 221184 | tf_op jit(solution)/shard_map/all_gather | solution.py:143
  343.7 5.4 %multiply_reduce_fusion = f32[16,256,128]{2,1,0:T(8,128)S(1)} fusion(f32[4,16,256,128]{3,2,1,0:T(8,128)} %all-to-all-done, f32[4,16,256]{2,1,0:T(8,128)S(1)} %get-tuple-element.181), kind=kLoop, calls=%fused_computation.28 | loop fusion | flops 3670016 | bytes 10551296 | tf_op jit(solution)/shard_map/reduce_sum | solution.py:41
  (112 shorter events, 61.3 us)
Async XLA Ops:
  7.2 40.4 %all-gather.5.cloned.1.call-start = ((), (), s32[]{:S(2)}) async-start(), calls=%async_computation.3 | async-start | bytes 5242880 | tf_op jit(solution)/shard_map/all_gather | solution.py:78
  9.5 12.4 %collective-permute-start = (bf16[2,2048]{1,0:T(2,128)(2,1)}, bf16[2,2048]{1,0:T(2,128)(2,1)S(1)}, u32[]{:S(2)}, u32[]{:S(2)}) collective-permute-start(bf16[2,2048]{1,0:T(2,128)(2,1)} %param.14), channel_id=1, source_target_pairs={{0,1},{1,2},{2,3},{3,0},{4,5},{5,6},{6,7},{7,4},{8,9},{9,10},{10,1... | collective-permute-start | bytes 24584 | tf_op jit(solution)/shard_map/ppermute | solution.py:106
  10.0 7.7 %copy-start = (bf16[3,2,512,1024]{3,2,1,0:T(8,128)(2,1)S(1)}, bf16[3,2,512,1024]{3,2,1,0:T(8,128)(2,1)}, u32[]{:S(2)}) copy-start(bf16[3,2,512,1024]{3,2,1,0:T(8,128)(2,1)} %param.15) | copy-start | bytes 18874372
  17.7 3.5 copy-start.7
  21.9 17.7 %collective-permute-start.1 = (bf16[2,2048]{1,0:T(2,128)(2,1)S(1)}, bf16[2,2048]{1,0:T(2,128)(2,1)S(1)}, u32[]{:S(2)}, u32[]{:S(2)}) collective-permute-start(bf16[2,2048]{1,0:T(2,128)(2,1)S(1)} %collective-permute-done), channel_id=1, source_target_pairs={{0,1},{1,2},{2,3},{3,0},{4,5},{5,6},{6,7},{7,4},{8,9},{9,10},{10,1... | collective-permute-start | bytes 24584 | tf_op jit(solution)/shard_map/ppermute | solution.py:106
  39.6 90.6 %collective-permute-start.2 = (bf16[2,2048]{1,0:T(2,128)(2,1)S(1)}, bf16[2,2048]{1,0:T(2,128)(2,1)S(1)}, u32[]{:S(2)}, u32[]{:S(2)}) collective-permute-start(bf16[2,2048]{1,0:T(2,128)(2,1)S(1)} %collective-permute-done.1), channel_id=1, source_target_pairs={{0,1},{1,2},{2,3},{3,0},{4,5},{5,6},{6,7},{7,4},{8,9},{9,10},{10,1... | collective-permute-start | bytes 24584 | tf_op jit(solution)/shard_map/ppermute | solution.py:106
  127.0 7.4 %all-to-all-start.2 = ((f32[4,16,256]{2,1,0:T(8,128)}), f32[4,16,256]{2,1,0:T(8,128)S(1)}, u32[]{:S(2)}, u32[]{:S(2)}) async-start(f32[4,16,256]{2,1,0:T(8,128)} %bitcast.13), calls=%async_computation.2 | async-start | bytes 131072 | tf_op jit(solution)/shard_map/all_to_all | solution.py:93
  134.3 0.6 copy-start.3
  135.0 7.4 %all-to-all-start.1 = ((f32[4,16,256]{2,1,0:T(8,128)}), f32[4,16,256]{2,1,0:T(8,128)S(1)}, u32[]{:S(2)}, u32[]{:S(2)}) async-start(f32[4,16,256]{2,1,0:T(8,128)} %bitcast.11), calls=%async_computation.1 | async-start | bytes 131072 | tf_op jit(solution)/shard_map/all_to_all | solution.py:92
  142.4 0.6 copy-start.1
  142.4 6.3 %copy-start.5 = (bf16[2,2048]{1,0:T(2,128)(2,1)S(1)}, bf16[2,2048]{1,0:T(2,128)(2,1)}, u32[]{:S(2)}) copy-start(bf16[2,2048]{1,0:T(2,128)(2,1)} %param.14) | copy-start | bytes 24580
  143.0 200.7 %all-to-all-start = ((f32[4,16,256,128]{3,2,1,0:T(8,128)}), f32[4,16,256,128]{3,2,1,0:T(8,128)}, u32[]{:S(2)}, u32[]{:S(2)}) async-start(f32[4,16,256,128]{3,2,1,0:T(8,128)} %bitcast.131), calls=%async_computation | async-start | bytes 16777216 | tf_op jit(solution)/shard_map/all_to_all | solution.py:94
  185.4 157.3 %copy-start.6 = (pred[2,24]{1,0:T(4,128)(4,1)S(1)}, pred[2,24]{1,0:T(4,128)(4,1)}, u32[]{:S(2)}) copy-start(pred[2,24]{1,0:T(4,128)(4,1)} %broadcast_compare_fusion.2) | copy-start | bytes 148
  185.4 158.3 %copy-start.2 = (f32[4,16,256]{2,1,0:T(8,128)S(1)}, f32[4,16,256]{2,1,0:T(8,128)}, u32[]{:S(2)}) copy-start(f32[4,16,256]{2,1,0:T(8,128)} %copy-done.1) | copy-start | bytes 196612
  185.4 158.3 %copy-start.4 = (f32[4,16,256]{2,1,0:T(8,128)S(1)}, f32[4,16,256]{2,1,0:T(8,128)}, u32[]{:S(2)}) copy-start(f32[4,16,256]{2,1,0:T(8,128)} %copy-done.3) | copy-start | bytes 196612
Sparse Core Ops, SparseCore 0:
  10.1 37.3 all-gather.4
